TPU v7x, 32 devices: a whole 2x2x4 slice. The times are simulated.
32 devices in a mesh: section: 2 (over core), dp: 16 (over z, y, x).
Axes of the slice: x: 2, y: 2, z: 4, core: 2. Of those that a mesh axis runs over, the one named last changes fastest.
Arguments:
- tokens: bfloat16 [2, 16, 128, 768], P(None, 'dp'), may hold values from -6 to 6
- cotangent: bfloat16 [2, 16, 128, 768], P(None, 'dp'), may hold values from -6 to 6
- lengths: int32 [2, 16], P(None, 'dp'), may hold values from 16 to 128, as said below
- qkv_weight: bfloat16 [2, 768, 2304], P('section', 'dp'), may hold values from -0.21875 to 0.21875
- out_weight: bfloat16 [2, 768, 768], P('section', 'dp'), may hold values from -1.75 to 1.75
- up_weight: bfloat16 [2, 768, 3072], P('section', 'dp'), may hold values from -0.21875 to 0.21875
- down_weight: bfloat16 [2, 3072, 768], P('section', 'dp'), may hold values from -0.109375 to 0.109375
- up_bias: bfloat16 [2, 3072], P('section', 'dp'), may hold values from -1.75 to 1.75
- norm_gains: bfloat16 [2, 2, 768], P('section', None, 'dp'), may hold values from 0.25 to 1.75
- biases: bfloat16 [2, 6, 768], P('section', None, 'dp'), may hold values from -1.75 to 1.75
Outputs:
- layer_outputs: bfloat16 [2, 2, 16, 128, 768], P('section', None, 'dp')
- input_grads: float32 [2, 2, 16, 128, 768], P('section', None, 'dp')
- qkv_grad: float32 [2, 768, 2304], P('section', 'dp')
- out_grad: float32 [2, 768, 768], P('section', 'dp')
- up_grad: float32 [2, 768, 3072], P('section', 'dp')
- down_grad: float32 [2, 3072, 768], P('section', 'dp')
- up_bias_grad: float32 [2, 3072], P('section', 'dp')
- gains_grad: float32 [2, 2, 768], P('section', None, 'dp')
- biases_grad: float32 [2, 6, 768], P('section', None, 'dp')
Inputs may be any that keep to these rules, and one draw needn't show every extreme that they name: `lengths`: in every draw some clip has all 128 frames valid.
All inputs are finite; a program needn't handle non-finite values.
Results may differ from a plain program's by a relative error of at most 0.017.
Values may be sent and summed in bfloat16 or wider, within the bound.
A program may use at most 320 MiB of HBM per device.

v0:
```python
import math

import jax
import jax.numpy as jnp
from jax import lax
from jax.sharding import PartitionSpec as P

HD = 64


EPSILON = 1e-05
MASKED = -1e30


def passed_along(shard, axis, by):
    length = lax.axis_size(axis)
    pairs = [(i, i + by) for i in range(length) if 0 <= i + by < length]
    return lax.ppermute(shard, axis, pairs)


def contract_rows(left, right):
    return lax.dot_general(
        left, right, (((0,), (0,)), ((), ())), preferred_element_type=jnp.float32
    )


def contract_cols(left, right):
    return lax.dot_general(
        left, right, (((1,), (1,)), ((), ())), preferred_element_type=jnp.float32
    )


def layer_norm(values, scale_gain, offset):
    average = jnp.mean(values, -1, keepdims=True)
    centred = values - average
    variance = jnp.mean(centred * centred, -1, keepdims=True)
    inverse = lax.rsqrt(variance + EPSILON)
    standard = centred * inverse
    return (standard * scale_gain + offset, standard, inverse)


def norm_backward(grad_out, standard, inverse, scale_gain):
    gain_grad = jnp.sum(grad_out * standard, 0)
    offset_grad = jnp.sum(grad_out, 0)
    scaled = grad_out * scale_gain
    values_grad = inverse * (
        scaled
        - jnp.mean(scaled, -1, keepdims=True)
        - standard * jnp.mean(scaled * standard, -1, keepdims=True)
    )
    return (values_grad, gain_grad, offset_grad)


def exact_gelu(values):
    return jax.nn.gelu(values, approximate=False)


def build_plan(micro_count):
    leading = [("F", 0)]
    for micro in range(micro_count):
        if micro + 1 < micro_count:
            leading.append(("F", micro + 1))
        leading.append(("B", micro))
    trailing = []
    for micro in range(micro_count):
        trailing.append(("F", micro))
        trailing.append(("B", micro))
    orders = (leading, trailing)
    finished = {}
    positions = [0, 0]
    table = []
    moment = 0
    while positions[0] < len(leading) or positions[1] < len(trailing):
        current = []
        for section_number in range(2):
            action = None
            if positions[section_number] < len(orders[section_number]):
                kind_name, micro = orders[section_number][positions[section_number]]
                needed = None
                if section_number == 0 and kind_name == "B":
                    needed = (1, "B", micro)
                if section_number == 1 and kind_name == "F":
                    needed = (0, "F", micro)
                if needed is None or finished.get(needed, moment) < moment:
                    action = (kind_name, micro)
            current.append(action)
        for section_number in range(2):
            action = current[section_number]
            if action is not None:
                finished[section_number, action[0], action[1]] = moment
                positions[section_number] += 1
        table.append(current)
        moment += 1
    return table


def attend_forward(query, keyed, valued, length):
    frames = query.shape[0]
    heads = query.shape[1] // HD
    block_rows = min(512, frames)
    scaling = 1.0 / math.sqrt(HD)
    query_blocks = query.reshape(frames // block_rows, block_rows, heads, HD)
    key_heads = keyed.reshape(frames, heads, HD)
    value_heads = valued.reshape(frames, heads, HD)
    visible = jnp.arange(frames) < length

    def one_block(query_block):
        scores = (
            jnp.einsum("qhd,khd->hqk", query_block, key_heads, preferred_element_type=jnp.float32)
            * scaling
        )
        scores = jnp.where(visible[None, None, :], scores, MASKED)
        largest = jnp.max(scores, -1, keepdims=True)
        exponent = jnp.exp(scores - largest)
        total = jnp.sum(exponent, -1, keepdims=True)
        probability = (exponent / total).astype(jnp.bfloat16)
        context = jnp.einsum(
            "hqk,khd->qhd", probability, value_heads, preferred_element_type=jnp.float32
        )
        return (context.astype(jnp.bfloat16), (largest + jnp.log(total))[..., 0])

    context, log_total = lax.map(one_block, query_blocks)
    return (context.reshape(frames, heads * HD), log_total)


def attend_backward(query, keyed, valued, log_total, context_grad, length):
    frames = query.shape[0]
    heads = query.shape[1] // HD
    block_rows = min(512, frames)
    scaling = 1.0 / math.sqrt(HD)
    query_blocks = query.reshape(frames // block_rows, block_rows, heads, HD)
    grad_blocks = context_grad.reshape(frames // block_rows, block_rows, heads, HD)
    key_heads = keyed.reshape(frames, heads, HD)
    value_heads = valued.reshape(frames, heads, HD)
    visible = jnp.arange(frames) < length

    def one_block(carry, record):
        key_grad, value_grad = carry
        query_block, grad_block, total_block = record
        scores = (
            jnp.einsum("qhd,khd->hqk", query_block, key_heads, preferred_element_type=jnp.float32)
            * scaling
        )
        scores = jnp.where(visible[None, None, :], scores, MASKED)
        probability = jnp.exp(scores - total_block[:, :, None])
        value_grad = value_grad + jnp.einsum(
            "hqk,qhd->khd",
            probability.astype(jnp.bfloat16),
            grad_block,
            preferred_element_type=jnp.float32,
        )
        prob_grad = jnp.einsum(
            "qhd,khd->hqk", grad_block, value_heads, preferred_element_type=jnp.float32
        )
        row_inner = jnp.sum(probability * prob_grad, -1, keepdims=True)
        score_grad = (probability * (prob_grad - row_inner)).astype(jnp.bfloat16)
        query_grad = (
            jnp.einsum("hqk,khd->qhd", score_grad, key_heads, preferred_element_type=jnp.float32)
            * scaling
        )
        key_grad = (
            key_grad
            + jnp.einsum(
                "hqk,qhd->khd", score_grad, query_block, preferred_element_type=jnp.float32
            )
            * scaling
        )
        return ((key_grad, value_grad), query_grad)

    empty = jnp.zeros((frames, heads, HD), jnp.float32)
    (key_grad, value_grad), query_grad = lax.scan(
        one_block, (empty, empty), (query_blocks, grad_blocks, log_total)
    )
    shape = (frames, heads * HD)
    return (query_grad.reshape(shape), key_grad.reshape(shape), value_grad.reshape(shape))


def layer_forward(source, length, weights):
    qkv_weight, out_weight, up_weight, down_weight, up_bias, norm_gains, biases = weights
    model_width = source.shape[1]
    inputs = source.astype(jnp.float32)
    normed = layer_norm(inputs, norm_gains[0], biases[0])[0].astype(jnp.bfloat16)
    mixed = jnp.dot(normed, qkv_weight, preferred_element_type=jnp.float32)
    query = (mixed[:, :model_width] + biases[1]).astype(jnp.bfloat16)
    keyed = mixed[:, model_width : 2 * model_width].astype(jnp.bfloat16)
    valued = (mixed[:, 2 * model_width :] + biases[2]).astype(jnp.bfloat16)
    context, log_total = attend_forward(query, keyed, valued, length)
    hidden = inputs + (jnp.dot(context, out_weight, preferred_element_type=jnp.float32) + biases[3])
    normed_two = layer_norm(hidden, norm_gains[1], biases[4])[0].astype(jnp.bfloat16)
    upper = jnp.dot(normed_two, up_weight, preferred_element_type=jnp.float32) + up_bias
    active = exact_gelu(upper).astype(jnp.bfloat16)
    result = hidden + (jnp.dot(active, down_weight, preferred_element_type=jnp.float32) + biases[5])
    saved = (
        source,
        normed,
        query,
        keyed,
        valued,
        log_total,
        context,
        hidden,
        normed_two,
        upper,
        active,
    )
    return (result, saved)


def blank_forward(frames, model_width, hidden_units, heads):
    block_rows = min(512, frames)
    zero_half = jnp.zeros((frames, model_width), jnp.bfloat16)
    zero_full = jnp.zeros((frames, model_width), jnp.float32)
    saved = (
        zero_half,
        zero_half,
        zero_half,
        zero_half,
        zero_half,
        jnp.zeros((frames // block_rows, heads, block_rows), jnp.float32),
        zero_half,
        zero_full,
        zero_half,
        jnp.zeros((frames, hidden_units), jnp.float32),
        jnp.zeros((frames, hidden_units), jnp.bfloat16),
    )
    return (zero_full, saved)


def layer_backward(grad_out, saved, length, weights):
    qkv_weight, out_weight, up_weight, down_weight, up_bias, norm_gains, biases = weights
    source, normed, query, keyed, valued, log_total, context, hidden, normed_two, upper, active = (
        saved
    )
    grad_half = grad_out.astype(jnp.bfloat16)
    down_term = contract_rows(active, grad_half)
    down_bias_term = jnp.sum(grad_half.astype(jnp.float32), 0)
    active_grad = contract_cols(grad_half, down_weight)
    gelu_back = jax.vjp(exact_gelu, upper)[1]
    upper_grad = gelu_back(active_grad)[0].astype(jnp.bfloat16)
    up_term = contract_rows(normed_two, upper_grad)
    up_bias_term = jnp.sum(upper_grad.astype(jnp.float32), 0)
    normed_two_grad = contract_cols(upper_grad, up_weight)
    second_std, second_inv = layer_norm(hidden, norm_gains[1], biases[4])[1:]
    hidden_part, second_gain, second_offset = norm_backward(
        normed_two_grad, second_std, second_inv, norm_gains[1]
    )
    hidden_grad = grad_out + hidden_part
    branch_grad = hidden_grad.astype(jnp.bfloat16)
    out_term = contract_rows(context, branch_grad)
    out_bias_term = jnp.sum(branch_grad.astype(jnp.float32), 0)
    context_grad = contract_cols(branch_grad, out_weight).astype(jnp.bfloat16)
    query_grad, key_grad, value_grad = attend_backward(
        query, keyed, valued, log_total, context_grad, length
    )
    query_grad = query_grad.astype(jnp.bfloat16)
    key_grad = key_grad.astype(jnp.bfloat16)
    value_grad = value_grad.astype(jnp.bfloat16)
    mixed_grad = jnp.concatenate([query_grad, key_grad, value_grad], 1)
    qkv_term = contract_rows(normed, mixed_grad)
    query_bias_term = jnp.sum(query_grad.astype(jnp.float32), 0)
    value_bias_term = jnp.sum(value_grad.astype(jnp.float32), 0)
    normed_grad = contract_cols(mixed_grad, qkv_weight)
    first_std, first_inv = layer_norm(source.astype(jnp.float32), norm_gains[0], biases[0])[1:]
    input_part, first_gain, first_offset = norm_backward(
        normed_grad, first_std, first_inv, norm_gains[0]
    )
    input_grad = hidden_grad + input_part
    gains_term = jnp.stack([first_gain, second_gain])
    biases_term = jnp.stack(
        [
            first_offset,
            query_bias_term,
            value_bias_term,
            out_bias_term,
            second_offset,
            down_bias_term,
        ]
    )
    return (
        input_grad,
        (qkv_term, out_term, up_term, down_term, up_bias_term, gains_term, biases_term),
    )


def store_where(buffer, slot, fresh, active_flag):
    return buffer.at[slot].set(jnp.where(active_flag, fresh, buffer[slot]))


def on_device(
    tokens,
    cotangent,
    lengths,
    qkv_weight,
    out_weight,
    up_weight,
    down_weight,
    up_bias,
    norm_gains,
    biases,
):
    section_index = lax.axis_index("section")
    is_first = section_index == 0
    micro_count = tokens.shape[0]
    frames = tokens.shape[2]
    model_width = tokens.shape[3]
    gathered = (
        lax.all_gather(qkv_weight, "dp", axis=1, tiled=True),
        lax.all_gather(out_weight, "dp", axis=1, tiled=True),
        lax.all_gather(up_weight, "dp", axis=1, tiled=True),
        lax.all_gather(down_weight, "dp", axis=1, tiled=True),
        lax.all_gather(up_bias, "dp", axis=1, tiled=True),
        lax.all_gather(norm_gains, "dp", axis=2, tiled=True),
        lax.all_gather(biases, "dp", axis=2, tiled=True),
    )
    weights = tuple((entry[0] for entry in gathered))
    hidden_units = weights[2].shape[1]
    heads = model_width // HD
    own_tokens = tokens[:, 0]
    own_cot = cotangent[:, 0]
    own_lengths = lengths[:, 0]

    def run_forward(source, length, layer_weights):
        return layer_forward(source, length, layer_weights)

    def skip_forward(source, length, layer_weights):
        return blank_forward(frames, model_width, hidden_units, heads)

    def run_backward(grad_in, saved, length, layer_weights):
        return layer_backward(grad_in, saved, length, layer_weights)

    def skip_backward(grad_in, saved, length, layer_weights):
        return (
            jnp.zeros((frames, model_width), jnp.float32),
            jax.tree.map(lambda entry: jnp.zeros(entry.shape, jnp.float32), layer_weights),
        )

    blank_saved = blank_forward(frames, model_width, hidden_units, heads)[1]
    saved_store = jax.tree.map(
        lambda entry: jnp.zeros((micro_count,) + entry.shape, entry.dtype), blank_saved
    )
    output_store = jnp.zeros((micro_count, frames, model_width), jnp.bfloat16)
    grad_store = jnp.zeros((micro_count, frames, model_width), jnp.float32)
    arrived_acts = jnp.zeros((micro_count, frames, model_width), jnp.bfloat16)
    arrived_grads = jnp.zeros((micro_count, frames, model_width), jnp.bfloat16)
    table = build_plan(micro_count)
    first_back = min(
        (
            moment
            for moment in range(len(table))
            if any((action is not None and action[0] == "B" for action in table[moment]))
        )
    )
    back_weights = weights
    gradients = jax.tree.map(lambda entry: jnp.zeros(entry.shape, jnp.float32), weights)
    early_owned = None
    for moment in range(len(table)):
        leading, trailing = table[moment]
        lead_forward = leading is not None and leading[0] == "F"
        trail_forward = trailing is not None and trailing[0] == "F"
        lead_backward = leading is not None and leading[0] == "B"
        trail_backward = trailing is not None and trailing[0] == "B"
        lead_micro = leading[1] if leading is not None else 0
        trail_micro = trailing[1] if trailing is not None else 0
        slot = jnp.where(is_first, lead_micro, trail_micro).astype(jnp.int32)
        length = lax.dynamic_index_in_dim(own_lengths, slot, 0, keepdims=False)
        if lead_forward or trail_forward:
            active_flag = jnp.where(is_first, lead_forward, trail_forward)
            source = jnp.where(is_first, own_tokens[lead_micro], arrived_acts[trail_micro])
            result, saved = lax.cond(
                active_flag, run_forward, skip_forward, source, length, weights
            )
            result_half = result.astype(jnp.bfloat16)
            saved_store = jax.tree.map(
                lambda buffer, fresh: store_where(buffer, slot, fresh, active_flag),
                saved_store,
                saved,
            )
            output_store = store_where(output_store, slot, result_half, active_flag)
            if lead_forward:
                received = passed_along(result_half, "section", 1)
                arrived_acts = arrived_acts.at[lead_micro].set(received)
        if lead_backward or trail_backward:
            if moment == first_back:
                regathered = (
                    lax.all_gather(qkv_weight, "dp", axis=1, tiled=True),
                    lax.all_gather(out_weight, "dp", axis=1, tiled=True),
                    lax.all_gather(up_weight, "dp", axis=1, tiled=True),
                    lax.all_gather(down_weight, "dp", axis=1, tiled=True),
                    lax.all_gather(up_bias, "dp", axis=1, tiled=True),
                    lax.all_gather(norm_gains, "dp", axis=2, tiled=True),
                    lax.all_gather(biases, "dp", axis=2, tiled=True),
                )
                back_weights = tuple((entry[0] for entry in regathered))
            active_flag = jnp.where(is_first, lead_backward, trail_backward)
            grad_in = jnp.where(is_first, arrived_grads[lead_micro], own_cot[trail_micro]).astype(
                jnp.float32
            )
            saved = jax.tree.map(
                lambda buffer: lax.dynamic_index_in_dim(buffer, slot, 0, keepdims=False),
                saved_store,
            )
            input_grad, step_grads = lax.cond(
                active_flag, run_backward, skip_backward, grad_in, saved, length, back_weights
            )
            gradients = jax.tree.map(jnp.add, gradients, step_grads)
            grad_store = store_where(grad_store, slot, input_grad, active_flag)
            if trail_backward:
                arriving = passed_along(input_grad.astype(jnp.bfloat16), "section", -1)
                arrived_grads = arrived_grads.at[trail_micro].set(arriving)
    owned = (
        lax.psum_scatter(gradients[0][None], "dp", scatter_dimension=1, tiled=True),
        lax.psum_scatter(gradients[1][None], "dp", scatter_dimension=1, tiled=True),
        lax.psum_scatter(gradients[2][None], "dp", scatter_dimension=1, tiled=True),
        lax.psum_scatter(gradients[3][None], "dp", scatter_dimension=1, tiled=True),
        lax.psum_scatter(gradients[4][None], "dp", scatter_dimension=1, tiled=True),
        lax.psum_scatter(gradients[5][None], "dp", scatter_dimension=2, tiled=True),
        lax.psum_scatter(gradients[6][None], "dp", scatter_dimension=2, tiled=True),
    )
    out_shape = (1, micro_count, 1, frames, model_width)
    return (
        output_store.reshape(out_shape),
        grad_store.reshape(out_shape),
        owned[0],
        owned[1],
        owned[2],
        owned[3],
        owned[4],
        owned[5],
        owned[6],
    )


def solution(mesh):
    placed = (
        P(None, "dp", None, None),
        P(None, "dp", None, None),
        P(None, "dp"),
        P("section", "dp", None),
        P("section", "dp", None),
        P("section", "dp", None),
        P("section", "dp", None),
        P("section", "dp"),
        P("section", None, "dp"),
        P("section", None, "dp"),
    )
    return jax.shard_map(
        on_device,
        mesh=mesh,
        in_specs=placed,
        out_specs=(
            P("section", None, "dp", None, None),
            P("section", None, "dp", None, None),
            P("section", "dp", None),
            P("section", "dp", None),
            P("section", "dp", None),
            P("section", "dp", None),
            P("section", "dp"),
            P("section", None, "dp"),
            P("section", None, "dp"),
        ),
        check_vma=False,
    )
```

profile of v0, /device:TPU:0, one launch (start us, length us, event | category | flops | bytes accessed | tf_op | source)
XLA Modules:
  0.0 1671.6 jit_solution(15800797116902244031)
XLA Ops:
  10.9 44.9 %all_gather.26 = bf16[1,2,768]{1,0,2:T(2,128)(2,1)S(1)} all-gather(bf16[1,2,48]{1,0,2:T(2,128)(2,1)S(1)} %copy.227), channel_id=1, replica_groups=mesh['section'=2,'dp'=16] {'dp'}, dimensions={2}, use_global_device_ids=true | all-gather | bytes 3264 | tf_op jit(solution)/shard_map/all_gather | solution.py:312
  56.2 38.7 %all_gather.27 = bf16[1,6,768]{1,0,2:T(2,128)(2,1)S(1)} all-gather(bf16[1,6,48]{1,0,2:T(2,128)(2,1)S(1)} %copy.229), channel_id=1, replica_groups=mesh['section'=2,'dp'=16] {'dp'}, dimensions={2}, use_global_device_ids=true | all-gather | bytes 9792 | tf_op jit(solution)/shard_map/all_gather | solution.py:313
  96.7 39.6 %all-reduce.14 = bf16[3072]{0:T(1024)(128)(2,1)S(1)} all-reduce(bf16[3072]{0:T(1024)(128)(2,1)S(1)} %dynamic-update-slice.139), channel_id=1, replica_groups=mesh['section'=2,'dp'=16] {'dp'}, use_global_device_ids=true, to_apply=%add.14 | all-reduce | flops 3072 | bytes 12288 | tf_op jit(solution)/shard_map/squeeze | solution.py:315
  145.7 13.4 fusion.282
  159.1 67.7 %all-gather.9.cloned.1.call-done = bf16[1,768,3072]{2,1,0:T(8,128)(2,1)} async-done(((bf16[1,48,3072]{2,1,0:T(8,128)(2,1)}), bf16[1,768,3072]{2,1,0:T(8,128)(2,1)}) %all-gather.9.cloned.1.call-update) | async-done | bytes 4718608 | tf_op jit(solution)/shard_map/all_gather | solution.py:309
  226.8 81.8 %all-gather.11.cloned.1.call-done = bf16[1,3072,768]{2,1,0:T(8,128)(2,1)} async-done(((bf16[1,192,768]{2,1,0:T(8,128)(2,1)}), bf16[1,3072,768]{2,1,0:T(8,128)(2,1)}) %all-gather.11.cloned.1.call-update) | async-done | bytes 4718608 | tf_op jit(solution)/shard_map/all_gather | solution.py:310
  308.6 22.8 %conditional.6 = (bf16[128,768]{1,0:T(8,128)(2,1)S(1)}, bf16[128,768]{1,0:T(8,128)(2,1)S(1)}, bf16[128,768]{1,0:T(8,128)(2,1)S(1)}, bf16[128,768]{1,0:T(8,128)(2...) conditional(s32[]{:T(128)} %convert_element_type.675, ...), branch_computations={%region_0.1_spmd, %region_1.8_spmd} | conditional | flops 1893048192 | bytes 57179932 | solution.py:369
  320.3 7.4 fusion.2
  332.6 17.8 %collective-permute-start = (bf16[128,768]{1,0:T(8,128)(2,1)}, bf16[128,768]{1,0:T(8,128)(2,1)S(1)}, u32[]{:S(2)}, u32[]{:S(2)}) collective-permute-start(bf16[128,768]{1,0:T(8,128)(2,1)} %get-tuple-element.1331), channel_id=1, source_target_pairs={{0,16},{1,17},{2,18},{3,19},{4,20},{5,21},{6,22},{7,23},{8,24},{9,... | collective-permute-start | bytes 589832 | tf_op jit(solution)/shard_map/ppermute | solution.py:18
  382.5 8.4 fusion.274
  407.1 11.5 conditional.8
  424.1 8.0 conditional.7
  462.0 19.2 %conditional.10 = (f32[128,768]{1,0:T(8,128)}, f32[3072,768]{1,0:T(8,128)S(1)}, f32[3072]{0:T(1024)S(1)}, f32[2,768]{1,0:T(2,128)S(1)}, f32[6,768]{1,0:T(8,128)S...) conditional(s32[]{:T(128)} %convert_element_type.705, () %tuple.269, ...), branch_computations={%region_66.67_spmd, %region_67.0_spmd} | conditional | flops 3790595072 | bytes 135854784 | solution.py:402
  485.2 66.2 %conditional.9 = (f32[128,768]{1,0:T(8,128)}, f32[3072,768]{1,0:T(8,128)S(1)}, f32[3072]{0:T(1024)}, f32[2,768]{1,0:T(2,128)S(1)}, f32[6,768]{1,0:T(8,128)S(1)},...) conditional(s32[]{:T(128)} %convert_element_type.675, () %tuple.267, ...), branch_computations={%region_46.47_spmd, %region_47.66_spmd} | conditional | flops 3790595072 | bytes 139037568 | solution.py:402
  485.5 8.3 convert_reduce_fusion.17
  512.9 8.4 copy.295
  538.9 9.7 copy.299
  551.3 50.9 %collective-permute-done.3 = bf16[128,768]{1,0:T(8,128)(2,1)} collective-permute-done((bf16[128,768]{1,0:T(8,128)(2,1)}, bf16[128,768]{1,0:T(8,128)(2,1)}, u32[]{:S(2)}, u32[]{:S(2)}) %collective-permute-start.3) | collective-permute-done | bytes 196640 | tf_op jit(solution)/shard_map/ppermute | solution.py:18
  603.4 41.6 %conditional.11 = (f32[128,768]{1,0:T(8,128)}, f32[768,2304]{1,0:T(8,128)}, f32[768,768]{1,0:T(8,128)}, f32[768,3072]{1,0:T(8,128)}, f32[3072,768]{1,0:T(8,128)}...) conditional(s32[]{:T(128)} %convert_element_type.675, () %tuple.270, ...), branch_computations={%region_86.87_spmd, %region_87.106_spmd} | conditional | flops 3790595072 | bytes 112338792 | solution.py:402
  604.3 8.5 convert_reduce_fusion.33
  638.6 6.1 fusion.194
  656.2 5.1 add_bitcast_fusion.5
  661.4 13.2 add_bitcast_fusion.4
  674.7 16.9 %add_bitcast_fusion.2 = f32[1,3072,768]{2,1,0:T(8,128)} fusion(f32[3072,768]{1,0:T(8,128)} %get-tuple-element.1374, f32[3072,768]{1,0:T(8,128)} %copy-done.2, f32[3072,768]{1,0:T(8,128)} %copy-done.4, f32[3072,768]{1,0:T(8,128)} %copy-done.3), kind=kLoop, calls=%fused_computation.509 | loop fusion | flops 7077888 | bytes 47185920 | tf_op jit(solution)/shard_map/broadcast_in_dim | solution.py:414
  691.7 17.4 %add_bitcast_fusion.3 = f32[1,768,3072]{2,1,0:T(8,128)} fusion(f32[768,3072]{1,0:T(8,128)} %get-tuple-element.1370, f32[768,3072]{1,0:T(8,128)} %get-tuple-element.1808, f32[768,3072]{1,0:T(8,128)} %get-tuple-element.1802, f32[768,3072]{1,0:T(8,128)} %get-tuple-element.1805), kind=kLoop, calls=%fused_computation.510 | loop fusion | flops 7077888 | bytes 47185920 | tf_op jit(solution)/shard_map/broadcast_in_dim | solution.py:413
  715.1 53.0 %reduce-scatter.24.cloned.1.call-done = f32[48,2]{1,0:T(8,128)} async-done(((f32[768,2]{1,0:T(8,128)}), f32[48,2]{1,0:T(8,128)}) %reduce-scatter.24.cloned.1.call-update) | async-done | bytes 400
  769.4 127.7 %reduce-scatter.22.cloned.1.call-done = f32[192,1]{1,0:T(8,128)} async-done(((f32[3072,1]{1,0:T(8,128)}), f32[192,1]{1,0:T(8,128)}) %reduce-scatter.22.cloned.1.call-update) | async-done | bytes 784
  898.7 124.4 %reduce-scatter.26.cloned.1.call-done = f32[48,6]{1,0:T(8,128)} async-done(((f32[768,6]{1,0:T(8,128)}), f32[48,6]{1,0:T(8,128)}) %reduce-scatter.26.cloned.1.call-update) | async-done | bytes 1168
  1024.6 130.7 %reduce-scatter.16.cloned.1.call-done = f32[1,48,768]{2,1,0:T(8,128)} async-done(((f32[1,768,768]{2,1,0:T(8,128)}), f32[1,48,768]{2,1,0:T(8,128)}) %reduce-scatter.16.cloned.1.call-update) | async-done | bytes 147472 | tf_op jit(solution)/shard_map/reduce_scatter | solution.py:412
  1155.2 156.2 %reduce-scatter.14.cloned.1.call-done = f32[1,48,2304]{2,1,0:T(8,128)} async-done(((f32[1,768,2304]{2,1,0:T(8,128)}), f32[1,48,2304]{2,1,0:T(8,128)}) %reduce-scatter.14.cloned.1.call-update) | async-done | bytes 442384 | tf_op jit(solution)/shard_map/reduce_scatter | solution.py:411
  1311.4 177.4 %reduce-scatter.20.cloned.1.call-done = f32[1,192,768]{2,1,0:T(8,128)} async-done(((f32[1,3072,768]{2,1,0:T(8,128)}), f32[1,192,768]{2,1,0:T(8,128)}) %reduce-scatter.20.cloned.1.call-update) | async-done | bytes 589840 | tf_op jit(solution)/shard_map/reduce_scatter | solution.py:414
  1488.8 176.0 %reduce-scatter.18.cloned.1.call-done = f32[1,48,3072]{2,1,0:T(8,128)} async-done(((f32[1,768,3072]{2,1,0:T(8,128)}), f32[1,48,3072]{2,1,0:T(8,128)}) %reduce-scatter.18.cloned.1.call-update) | async-done | bytes 589840 | tf_op jit(solution)/shard_map/reduce_scatter | solution.py:413
  (518 shorter events, 236.0 us)
Async XLA Ops:
  7.2 88.0 %copy-start.127 = (u32[32]{0:T(128)S(1)}, u32[32]{0:T(128)}, u32[]{:S(2)}) copy-start(u32[32]{0:T(128)} %constant.2013) | copy-start | bytes 388
  7.2 131.5 %copy-start.125 = (s32[3]{0:T(128)S(1)}, s32[3]{0:T(128)}, u32[]{:S(2)}) copy-start(s32[3]{0:T(128)} %constant.1935.clone.1) | copy-start | bytes 40
  7.2 132.2 %copy-start.124 = (s32[4]{0:T(128)S(1)}, s32[4]{0:T(128)}, u32[]{:S(2)}) copy-start(s32[4]{0:T(128)} %constant.1972.clone.1) | copy-start | bytes 52
  7.2 48.9 %copy-start.121 = (bf16[1,6,48]{2,1,0:T(8,128)(2,1)S(1)}, bf16[1,6,48]{2,1,0:T(8,128)(2,1)}, u32[]{:S(2)}) copy-start(bf16[1,6,48]{2,1,0:T(8,128)(2,1)} %param.119) | copy-start | bytes 1732
  7.2 89.2 %copy-start.122 = (bf16[1,192]{1,0:T(2,128)(2,1)S(1)}, bf16[1,192]{1,0:T(2,128)(2,1)}, u32[]{:S(2)}) copy-start(bf16[1,192]{1,0:T(2,128)(2,1)} %param.117) | copy-start | bytes 1156
  7.2 129.7 %copy-start.120 = (s32[2,1]{0,1:T(1,128)S(1)}, s32[2,1]{0,1:T(1,128)}, u32[]{:S(2)}) copy-start(s32[2,1]{0,1:T(1,128)} %param.112) | copy-start | bytes 28
  7.2 151.8 %all-gather.7.cloned.1.call-start = ((), (), s32[]{:S(2)}) async-start(), calls=%async_computation.8 | async-start | bytes 1253376 | tf_op jit(solution)/shard_map/all_gather | solution.py:308
  8.0 151.1 %all-gather.5.cloned.1.call-start = ((), (), s32[]{:S(2)}) async-start(), calls=%async_computation.7 | async-start | bytes 3760128 | tf_op jit(solution)/shard_map/all_gather | solution.py:307
  8.7 136.1 %copy-start.80 = (bf16[2,1,128,768]{3,2,1,0:T(8,128)(2,1)S(1)}, bf16[2,1,128,768]{3,2,1,0:T(8,128)(2,1)}, u32[]{:S(2)}) copy-start(bf16[2,1,128,768]{3,2,1,0:T(8,128)(2,1)} %param.110) | copy-start | bytes 1179652
  8.7 218.1 %all-gather.9.cloned.1.call-start = ((), (), s32[]{:S(2)}) async-start(), calls=%async_computation.9 | async-start | bytes 5013504 | tf_op jit(solution)/shard_map/all_gather | solution.py:309
  9.5 135.4 %copy-start.82 = (bf16[2,1,128,768]{3,2,1,0:T(8,128)(2,1)S(1)}, bf16[2,1,128,768]{3,2,1,0:T(8,128)(2,1)}, u32[]{:S(2)}) copy-start(bf16[2,1,128,768]{3,2,1,0:T(8,128)(2,1)} %param.111) | copy-start | bytes 1179652
  9.5 299.1 %all-gather.11.cloned.1.call-start = ((), (), s32[]{:S(2)}) async-start(), calls=%async_computation.10 | async-start | bytes 5013504 | tf_op jit(solution)/shard_map/all_gather | solution.py:310
  10.1 758.0 %reduce-scatter.24.cloned.1.call-start = ((), (), s32[]{:S(2)}) async-start(), calls=%async_computation.16 | async-start | bytes 417792
  144.8 163.8 %copy-start.74 = (bf16[128,768]{1,0:T(8,128)(2,1)}, bf16[128,768]{1,0:T(8,128)(2,1)S(1)}, u32[]{:S(2)}) copy-start(bf16[128,768]{1,0:T(8,128)(2,1)S(1)} %slice_bitcast_fusion.1) | copy-start | bytes 589828
  332.6 30.3 %collective-permute-start = (bf16[128,768]{1,0:T(8,128)(2,1)}, bf16[128,768]{1,0:T(8,128)(2,1)S(1)}, u32[]{:S(2)}, u32[]{:S(2)}) collective-permute-start(bf16[128,768]{1,0:T(8,128)(2,1)} %get-tuple-element.1331), channel_id=1, source_target_pairs={{0,16},{1,17},{2,18},{3,19},{4,20},{5,21},{6,22},{7,23},{8,24},{9,... | collective-permute-start | bytes 589832 | tf_op jit(solution)/shard_map/ppermute | solution.py:18
  378.2 12.6 slice-start.8
  382.5 14.2 copy-start.31
  390.9 16.1 slice-start
  393.1 30.9 %collective-permute-start.1 = (bf16[128,768]{1,0:T(8,128)(2,1)}, bf16[128,768]{1,0:T(8,128)(2,1)}, u32[]{:S(2)}, u32[]{:S(2)}) collective-permute-start(bf16[128,768]{1,0:T(8,128)(2,1)} %get-tuple-element.2008), channel_id=1, source_target_pairs={{0,16},{1,17},{2,18},{3,19},{4,20},{5,21},{6,22},{7,23},{8,24},{9,... | collective-permute-start | bytes 589832 | tf_op jit(solution)/shard_map/ppermute | solution.py:18
  422.0 38.3 %collective-permute-start.2 = (bf16[128,768]{1,0:T(8,128)(2,1)}, bf16[128,768]{1,0:T(8,128)(2,1)}, u32[]{:S(2)}, u32[]{:S(2)}) collective-permute-start(bf16[128,768]{1,0:T(8,128)(2,1)} %get-tuple-element.1997), channel_id=1, source_target_pairs={{16,0},{17,1},{18,2},{19,3},{20,4},{21,5},{22,6},{23,7},{24,8},{25... | collective-permute-start | bytes 589832 | tf_op jit(solution)/shard_map/ppermute | solution.py:18
  483.8 118.4 %collective-permute-start.3 = (bf16[128,768]{1,0:T(8,128)(2,1)}, bf16[128,768]{1,0:T(8,128)(2,1)}, u32[]{:S(2)}, u32[]{:S(2)}) collective-permute-start(bf16[128,768]{1,0:T(8,128)(2,1)} %convert_element_type.711), channel_id=1, source_target_pairs={{16,0},{17,1},{18,2},{19,3},{20,4},{21,5},{22,6},{23,7},{24,8},{25... | collective-permute-start | bytes 589832 | tf_op jit(solution)/shard_map/ppermute | solution.py:18
  551.3 52.0 %copy-start.3 = (f32[3072,768]{1,0:T(8,128)}, f32[3072,768]{1,0:T(8,128)S(1)}, u32[]{:S(2)}) copy-start(f32[3072,768]{1,0:T(8,128)S(1)} %get-tuple-element.1372) | copy-start | bytes 28311556
  551.3 52.0 %copy-start.110 = (f32[2,768]{1,0:T(2,128)}, f32[2,768]{1,0:T(2,128)S(1)}, u32[]{:S(2)}) copy-start(f32[2,768]{1,0:T(2,128)S(1)} %get-tuple-element.1380) | copy-start | bytes 18436
  603.3 44.3 %copy-start.106 = (f32[3072]{0:T(1024)S(1)}, f32[3072]{0:T(1024)}, u32[]{:S(2)}) copy-start(f32[3072]{0:T(1024)} %copy-done.105) | copy-start | bytes 36868
  646.8 250.4 %reduce-scatter.22.cloned.1.call-start = ((), (), s32[]{:S(2)}) async-start(), calls=%async_computation.15 | async-start | bytes 1671168
  652.4 370.7 %reduce-scatter.26.cloned.1.call-start = ((), (), s32[]{:S(2)}) async-start(), calls=%async_computation.17 | async-start | bytes 417792
  656.1 499.1 %reduce-scatter.16.cloned.1.call-start = ((), (), s32[]{:S(2)}) async-start(), calls=%async_computation.12 | async-start | bytes 2506752 | tf_op jit(solution)/shard_map/reduce_scatter | solution.py:412
  661.4 650.1 %reduce-scatter.14.cloned.1.call-start = ((), (), s32[]{:S(2)}) async-start(), calls=%async_computation.11 | async-start | bytes 7520256 | tf_op jit(solution)/shard_map/reduce_scatter | solution.py:411
  674.6 814.1 %reduce-scatter.20.cloned.1.call-start = ((), (), s32[]{:S(2)}) async-start(), calls=%async_computation.14 | async-start | bytes 10027008 | tf_op jit(solution)/shard_map/reduce_scatter | solution.py:414
  691.7 973.2 %reduce-scatter.18.cloned.1.call-start = ((), (), s32[]{:S(2)}) async-start(), calls=%async_computation.13 | async-start | bytes 10027008 | tf_op jit(solution)/shard_map/reduce_scatter | solution.py:413
  713.4 951.4 %copy-start.102 = (bf16[1,2,1,128,768]{4,3,1,2,0:T(8,128)(2,1)}, bf16[1,2,1,128,768]{4,3,1,2,0:T(8,128)(2,1)S(1)}, u32[]{:S(2)}) copy-start(bf16[1,2,1,128,768]{4,3,1,2,0:T(8,128)(2,1)S(1)} %bitcast_dynamic-update-slice_fusion.1) | copy-start | bytes 1179652
  715.1 949.8 %copy-start.88 = (f32[1,2,1,128,768]{4,3,1,2,0:T(8,128)}, f32[1,2,1,128,768]{4,3,1,2,0:T(8,128)S(1)}, u32[]{:S(2)}) copy-start(f32[1,2,1,128,768]{4,3,1,2,0:T(8,128)S(1)} %bitcast_dynamic-update-slice_fusion) | copy-start | bytes 2359300
  (95 other events, 404.8 us)
Sparse Core Ops, SparseCore 0:
  10.9 60.1 all-gather.6
  73.8 70.8 all-gather.4
  147.5 79.3 all-gather.8
  229.5 79.0 all-gather.10
  646.9 121.1 reduce-scatter.23
  773.4 123.6 reduce-scatter.21
  902.5 120.4 reduce-scatter.25
  1028.5 126.7 reduce-scatter.15
  1162.0 149.3 reduce-scatter.13
  1318.5 170.2 reduce-scatter.19
  1495.0 169.7 reduce-scatter.17
where the time goes:
time: 1680 us; the launch traced here: 1670 us
  waiting for transfers between devices  1150 us (68%)
  other arithmetic  136 us (8%)
  blocking collectives  123 us (7%)
  local copies, waits for them, and re-layouts  121 us (7%)
  matrix products  94.2 us (6%)
  starting transfers between devices  22.7 us (1%)
    unnamed x14, waiting for transfers between devices  308 us
    reduce_scatter x1, waiting for transfers between devices, on_device(): lax.psum_scatter(gradients[3][None], 'dp', scatter_dimension=1, tiled=True)  177 us
    reduce_scatter x1, waiting for transfers between devices, on_device(): lax.psum_scatter(gradients[2][None], 'dp', scatter_dimension=1, tiled=True)  176 us
    reduce_scatter x1, waiting for transfers between devices, on_device(): lax.psum_scatter(gradients[0][None], 'dp', scatter_dimension=1, tiled=True)  156 us
    reduce_scatter x1, waiting for transfers between devices, on_device(): lax.psum_scatter(gradients[1][None], 'dp', scatter_dimension=1, tiled=True)  131 us
    all_gather x1, waiting for transfers between devices, on_device(): lax.all_gather(down_weight, 'dp', axis=1, tiled=True)  81.8 us
    all_gather x1, waiting for transfers between devices, on_device(): lax.all_gather(up_weight, 'dp', axis=1, tiled=True)  67.7 us
    ppermute x4, waiting for transfers between devices, passed_along(): return lax.ppermute(shard, axis, pairs)  50.9 us
  transfers between devices with their start and end apart: 15, of which 10 were waited for; matrix products, arithmetic and copies ran while one was open for 14% of the time, Pallas kernels for 0%

commit v1 on v0

v1 whole, which is shorter than its diff:
```python
import functools
import math

import jax
import jax.numpy as jnp
from jax import lax
from jax.experimental import pallas as pl
from jax.experimental.pallas import tpu as pltpu
from jax.sharding import PartitionSpec as P

HD = 64
EPSILON = 1e-05
MASKED = -1e30
MESH = pl.DeviceIdType.MESH
F32 = jnp.float32
BF16 = jnp.bfloat16


def factor(count):
    side = 1
    while (2 * side) ** 3 <= count:
        side *= 2
    if count % (side * side):
        return (count, 1, 1)
    return (count // (side * side), side, side)


class Grid:
    def __init__(self, sizes):
        self.sizes = sizes
        slow, middle, fast = sizes
        me = lax.axis_index("dp")
        self.me = me
        self.z = me // (middle * fast)
        self.y = (me // fast) % middle
        self.x = me % fast

    def flat(self, z, y, x):
        return (z * self.sizes[1] + y) * self.sizes[2] + x

    def pair(self, z, y_first, a, b):
        return self.flat(z, a, b) if y_first else self.flat(z, b, a)

    def greet(self):
        slow, middle, fast = self.sizes
        barrier = pltpu.get_barrier_semaphore()
        peers = [self.flat((self.z + o) % slow, self.y, self.x) for o in range(1, slow)]
        peers += [self.flat(self.z, (self.y + o) % middle, self.x) for o in range(1, middle)]
        peers += [self.flat(self.z, self.y, (self.x + o) % fast) for o in range(1, fast)]
        for peer in peers:
            pl.semaphore_signal(barrier, inc=1, device_id={"dp": peer}, device_id_type=MESH)
        pl.semaphore_wait(barrier, len(peers))


def gather_kernel(sizes, count, *refs):
    shards, wholes = refs[:count], refs[count : 2 * count]
    send_sem, recv_sem, local_sem = refs[2 * count :]
    grid = Grid(sizes)
    slow = sizes[0]
    local = [
        pltpu.make_async_copy(shards[w], wholes[w].at[grid.me], local_sem.at[w])
        for w in range(count)
    ]
    for copy in local:
        copy.start()
    grid.greet()
    used = [0] * count
    sent = []

    def send(w, block, target):
        copy = pltpu.make_async_remote_copy(
            src_ref=wholes[w].at[block],
            dst_ref=wholes[w].at[block],
            send_sem=send_sem.at[w, used[w]],
            recv_sem=recv_sem.at[w, block],
            device_id={"dp": target},
            device_id_type=MESH,
        )
        copy.start()
        used[w] += 1
        sent.append(copy)

    def arrive(w, block):
        pltpu.make_async_remote_copy(
            src_ref=wholes[w].at[block],
            dst_ref=wholes[w].at[block],
            send_sem=send_sem.at[w, 0],
            recv_sem=recv_sem.at[w, block],
            device_id={"dp": grid.flat((grid.z + 1) % slow, grid.y, grid.x)},
            device_id_type=MESH,
        ).wait_recv()

    def place(z):
        y_first = z % 2 == 1
        if y_first:
            return True, grid.y, grid.x, sizes[1], sizes[2]
        return False, grid.x, grid.y, sizes[2], sizes[1]

    def first_stage(w):
        for z in range(slow):
            y_first, a, b, n_a, n_b = place(z)
            block = grid.flat(z, grid.y, grid.x)

            @pl.when(grid.z != z)
            def _():
                arrive(w, block)

            for o in range(1, n_a):
                send(w, block, grid.pair(grid.z, y_first, (a + o) % n_a, b))
            for o in range(1, n_b):
                send(w, block, grid.pair(grid.z, y_first, a, (b + o) % n_b))

    def second_stage(w):
        for z in range(slow):
            y_first, a, b, n_a, n_b = place(z)
            for o in range(1, n_a):
                block = grid.pair(z, y_first, (a + o) % n_a, b)
                arrive(w, block)
                for p in range(1, n_b):
                    send(w, block, grid.pair(grid.z, y_first, a, (b + p) % n_b))

    def third_stage(w):
        for z in range(slow):
            y_first, a, b, n_a, n_b = place(z)
            for o in range(n_a):
                for p in range(1, n_b):
                    arrive(w, grid.pair(z, y_first, (a + o) % n_a, (b + p) % n_b))

    for w in range(count):
        local[w].wait()
        for o in range(1, slow):
            send(w, grid.me, grid.flat((grid.z + o) % slow, grid.y, grid.x))
    for step in range(count + 1):
        if step < count:
            first_stage(step)
        if step >= 1:
            second_stage(step - 1)
    for w in range(count):
        third_stage(w)
    for copy in sent:
        copy.wait_send()


def gather_blocks(shards, sizes):
    total = sizes[0] * sizes[1] * sizes[2]
    count = len(shards)
    anywhere = pl.BlockSpec(memory_space=pl.ANY)
    return pl.pallas_call(
        functools.partial(gather_kernel, sizes, count),
        out_shape=[jax.ShapeDtypeStruct((total,) + s.shape, s.dtype) for s in shards],
        in_specs=[anywhere] * count,
        out_specs=[anywhere] * count,
        scratch_shapes=[
            pltpu.SemaphoreType.DMA((count, total)),
            pltpu.SemaphoreType.DMA((count, total)),
            pltpu.SemaphoreType.DMA((count,)),
        ],
        compiler_params=pltpu.CompilerParams(collective_id=0, has_side_effects=True),
        name="gather_blocks",
    )(*shards)


def scatter_kernel(sizes, count, *refs):
    terms, totals = refs[:count], refs[count : 2 * count]
    one, two, three = (refs[(2 + i) * count : (3 + i) * count] for i in range(3))
    send_sem, sem_one, sem_two, sem_three = refs[5 * count :]
    grid = Grid(sizes)
    slow = sizes[0]
    grid.greet()
    used = [0] * count
    sent = []

    def send(w, source, landing, semaphore, target):
        copy = pltpu.make_async_remote_copy(
            src_ref=source,
            dst_ref=landing,
            send_sem=send_sem.at[w, used[w]],
            recv_sem=semaphore,
            device_id={"dp": target},
            device_id_type=MESH,
        )
        copy.start()
        used[w] += 1
        sent.append(copy)

    def arrive(w, landing, semaphore):
        pltpu.make_async_remote_copy(
            src_ref=landing,
            dst_ref=landing,
            send_sem=send_sem.at[w, 0],
            recv_sem=semaphore,
            device_id={"dp": grid.flat((grid.z + 1) % slow, grid.y, grid.x)},
            device_id_type=MESH,
        ).wait_recv()

    def place(z):
        y_first = z % 2 == 0
        if y_first:
            return True, grid.y, grid.x, sizes[1], sizes[2]
        return False, grid.x, grid.y, sizes[2], sizes[1]

    def send_one(w):
        for z in range(slow):
            y_first, a, b, n_a, n_b = place(z)
            for o in range(1, n_a):
                far = (a + o) % n_a
                for p in range(n_b):
                    send(
                        w,
                        terms[w].at[grid.pair(z, y_first, far, p)],
                        one[w].at[z, o - 1, p],
                        sem_one.at[w, z, o - 1, p],
                        grid.pair(grid.z, y_first, far, b),
                    )

    def finish_one(w):
        for z in range(slow):
            y_first, a, b, n_a, n_b = place(z)
            for q in range(n_b):
                p = (b + 1 + q) % n_b
                for o in range(1, n_a):
                    arrive(w, one[w].at[z, o - 1, p], sem_one.at[w, z, o - 1, p])
                value = terms[w][grid.pair(z, y_first, a, p)].astype(F32)
                for o in range(1, n_a):
                    value = value + one[w][z, o - 1, p].astype(F32)
                one[w][z, 0, p] = value.astype(one[w].dtype)
                if q < n_b - 1:
                    send(
                        w,
                        one[w].at[z, 0, p],
                        two[w].at[z, q],
                        sem_two.at[w, z, q],
                        grid.pair(grid.z, y_first, a, p),
                    )

    def finish_two(w):
        for z in range(slow):
            y_first, a, b, n_a, n_b = place(z)
            for q in range(n_b - 1):
                arrive(w, two[w].at[z, q], sem_two.at[w, z, q])
            value = one[w][z, 0, b].astype(F32)
            for q in range(n_b - 1):
                value = value + two[w][z, q].astype(F32)
            two[w][z, 0] = value.astype(two[w].dtype)
        for o in range(1, slow):
            far = (grid.z + o) % slow
            send(
                w,
                two[w].at[far, 0],
                three[w].at[o - 1],
                sem_three.at[w, o - 1],
                grid.flat(far, grid.y, grid.x),
            )

    def finish_three(w):
        value = two[w][grid.z, 0].astype(F32)
        for o in range(1, slow):
            arrive(w, three[w].at[o - 1], sem_three.at[w, o - 1])
            value = value + three[w][o - 1].astype(F32)
        totals[w][...] = value

    for w in range(min(2, count)):
        send_one(w)
    for step in range(count + 2):
        if step < count:
            finish_one(step)
        if step + 2 < count:
            send_one(step + 2)
        if 1 <= step <= count:
            finish_two(step - 1)
        if step >= 2:
            finish_three(step - 2)
    for copy in sent:
        copy.wait_send()


def scatter_blocks(terms, sizes):
    slow, middle, fast = sizes
    total = slow * middle * fast
    count = len(terms)
    inside = pl.BlockSpec(memory_space=pltpu.VMEM)
    return pl.pallas_call(
        functools.partial(scatter_kernel, sizes, count),
        out_shape=[jax.ShapeDtypeStruct(t.shape[1:], F32) for t in terms],
        in_specs=[inside] * count,
        out_specs=[inside] * count,
        scratch_shapes=[
            pltpu.VMEM((slow, middle - 1, middle) + t.shape[1:], t.dtype) for t in terms
        ]
        + [pltpu.VMEM((slow, middle - 1) + t.shape[1:], t.dtype) for t in terms]
        + [pltpu.VMEM((slow - 1,) + t.shape[1:], t.dtype) for t in terms]
        + [
            pltpu.SemaphoreType.DMA((count, total)),
            pltpu.SemaphoreType.DMA((count, slow, middle - 1, middle)),
            pltpu.SemaphoreType.DMA((count, slow, middle - 1)),
            pltpu.SemaphoreType.DMA((count, slow - 1)),
        ],
        compiler_params=pltpu.CompilerParams(
            collective_id=1, has_side_effects=True, vmem_limit_bytes=48 * 1024 * 1024
        ),
        name="scatter_blocks",
    )(*terms)


def contract_rows(left, right):
    return lax.dot_general(left, right, (((0,), (0,)), ((), ())), preferred_element_type=F32)


def contract_cols(left, right):
    return lax.dot_general(left, right, (((1,), (1,)), ((), ())), preferred_element_type=F32)


def standardize(values):
    centred = values - jnp.mean(values, -1, keepdims=True)
    variance = jnp.mean(centred * centred, -1, keepdims=True)
    inverse = lax.rsqrt(variance + EPSILON)
    return centred * inverse, inverse


def norm_backward(grad_out, standard, inverse, gain):
    scaled = grad_out * gain
    return inverse * (
        scaled
        - jnp.mean(scaled, -1, keepdims=True)
        - standard * jnp.mean(scaled * standard, -1, keepdims=True)
    )


def normal_cdf(values):
    return 0.5 * (1.0 + lax.erf(values * math.sqrt(0.5)))


def by_head(values, clips):
    rows, width = values.shape
    return values.reshape(clips, rows // clips, width // HD, HD).transpose(0, 2, 1, 3)


def by_row(values):
    clips, heads, frames, size = values.shape
    return values.transpose(0, 2, 1, 3).reshape(clips * frames, heads * size)


def scores_of(query, keyed, visible):
    scores = jnp.einsum("chqd,chkd->chqk", query, keyed, preferred_element_type=F32)
    return jnp.where(visible, scores * (1.0 / math.sqrt(HD)), MASKED)


def layer_forward(source, visible, clips, weights):
    qkv_weight, out_weight, up_weight, down_weight, up_bias, gains, biases = weights
    width = source.shape[1]
    inputs = source.astype(F32)
    standard, inverse = standardize(inputs)
    normed = (standard * gains[0] + biases[0]).astype(BF16)
    mixed = jnp.dot(normed, qkv_weight, preferred_element_type=F32)
    query = by_head((mixed[:, :width] + biases[1]).astype(BF16), clips)
    keyed = by_head(mixed[:, width : 2 * width].astype(BF16), clips)
    valued = by_head((mixed[:, 2 * width :] + biases[2]).astype(BF16), clips)
    scores = scores_of(query, keyed, visible)
    largest = jnp.max(scores, -1, keepdims=True)
    exponent = jnp.exp(scores - largest)
    total = jnp.sum(exponent, -1, keepdims=True)
    probability = (exponent / total).astype(BF16)
    context = jnp.einsum("chqk,chkd->chqd", probability, valued, preferred_element_type=F32)
    context = by_row(context.astype(BF16))
    log_total = largest + jnp.log(total)
    hidden = inputs + (jnp.dot(context, out_weight, preferred_element_type=F32) + biases[3])
    standard_two, inverse_two = standardize(hidden)
    normed_two = (standard_two * gains[1] + biases[4]).astype(BF16)
    upper = jnp.dot(normed_two, up_weight, preferred_element_type=F32) + up_bias
    active = (upper * normal_cdf(upper)).astype(BF16)
    result = hidden + (jnp.dot(active, down_weight, preferred_element_type=F32) + biases[5])
    saved = (
        (standard, inverse, normed, query, keyed, valued, log_total, context)
        + (standard_two, inverse_two, normed_two, upper, active)
    )
    return result.astype(BF16), saved


def layer_backward(grad_half, saved, visible, clips, weights):
    qkv_weight, out_weight, up_weight, down_weight, up_bias, gains, biases = weights
    standard, inverse, normed, query, keyed, valued, log_total, context = saved[:8]
    standard_two, inverse_two, normed_two, upper, active = saved[8:]
    scaling = 1.0 / math.sqrt(HD)
    grad_out = grad_half.astype(F32)
    active_grad = contract_cols(grad_half, down_weight)
    density = jnp.exp(-0.5 * upper * upper) * (1.0 / math.sqrt(2.0 * math.pi))
    upper_grad = (active_grad * (normal_cdf(upper) + upper * density)).astype(BF16)
    normed_two_grad = contract_cols(upper_grad, up_weight)
    hidden_grad = grad_out + norm_backward(normed_two_grad, standard_two, inverse_two, gains[1])
    branch_grad = hidden_grad.astype(BF16)
    context_grad = by_head(contract_cols(branch_grad, out_weight).astype(BF16), clips)
    probability = jnp.exp(scores_of(query, keyed, visible) - log_total)
    value_grad = jnp.einsum(
        "chqk,chqd->chkd", probability.astype(BF16), context_grad, preferred_element_type=F32
    )
    prob_grad = jnp.einsum("chqd,chkd->chqk", context_grad, valued, preferred_element_type=F32)
    inner = jnp.sum(probability * prob_grad, -1, keepdims=True)
    score_grad = (probability * (prob_grad - inner)).astype(BF16)
    query_grad = scaling * jnp.einsum(
        "chqk,chkd->chqd", score_grad, keyed, preferred_element_type=F32
    )
    key_grad = scaling * jnp.einsum(
        "chqk,chqd->chkd", score_grad, query, preferred_element_type=F32
    )
    mixed_grad = jnp.concatenate(
        [by_row(part.astype(BF16)) for part in (query_grad, key_grad, value_grad)], 1
    )
    normed_grad = contract_cols(mixed_grad, qkv_weight)
    input_grad = hidden_grad + norm_backward(normed_grad, standard, inverse, gains[0])
    return input_grad, (upper_grad, normed_two_grad, branch_grad, mixed_grad, normed_grad)


def weight_terms(grad_half, saved, grads):
    standard, normed, context = saved[0], saved[2], saved[7]
    standard_two, normed_two, active = saved[8], saved[10], saved[12]
    upper_grad, normed_two_grad, branch_grad, mixed_grad, normed_grad = grads
    width = standard.shape[1]
    large = (
        contract_rows(normed, mixed_grad),
        contract_rows(context, branch_grad),
        contract_rows(normed_two, upper_grad),
        contract_rows(active, grad_half),
    )
    mixed_sum = jnp.sum(mixed_grad.astype(F32), 0)
    gains = jnp.stack(
        [jnp.sum(normed_grad * standard, 0), jnp.sum(normed_two_grad * standard_two, 0)]
    )
    biases = jnp.stack(
        [
            jnp.sum(normed_grad, 0),
            mixed_sum[:width],
            mixed_sum[2 * width :],
            jnp.sum(branch_grad.astype(F32), 0),
            jnp.sum(normed_two_grad, 0),
            jnp.sum(grad_half.astype(F32), 0),
        ]
    )
    return large, (jnp.sum(upper_grad.astype(F32), 0), gains, biases)


def gather_weights(large, small, sizes):
    total = sizes[0] * sizes[1] * sizes[2]
    if any(entry.shape[0] % 16 for entry in large) or min(sizes) < 2:
        return tuple(lax.all_gather(entry, "dp", axis=0, tiled=True) for entry in large) + tuple(
            lax.all_gather(entry, "dp", axis=entry.ndim - 1, tiled=True) for entry in small
        )
    flat = jnp.concatenate([entry.reshape(-1) for entry in small])
    room = -(-flat.size // 2048) * 2048
    packed = jnp.pad(flat, (0, room - flat.size)).reshape(-1, 128)
    *wholes, joined = gather_blocks(tuple(large[i] for i in (0, 1, 2, 3)) + (packed,), sizes)
    joined = joined.reshape(total, room)
    result = [whole.reshape(-1, whole.shape[2]) for whole in wholes]
    start = 0
    for entry in small:
        piece = joined[:, start : start + entry.size].reshape((total,) + entry.shape)
        result.append(jnp.moveaxis(piece, 0, -2).reshape(entry.shape[:-1] + (-1,)))
        start += entry.size
    return tuple(result)


def scatter_terms(large, small, sizes):
    total = sizes[0] * sizes[1] * sizes[2]
    if any((entry.shape[0] // total) % 16 for entry in large) or min(sizes) < 2:
        return tuple(
            lax.psum_scatter(entry, "dp", scatter_dimension=0, tiled=True) for entry in large
        ) + tuple(
            lax.psum_scatter(entry, "dp", scatter_dimension=entry.ndim - 1, tiled=True)
            for entry in small
        )
    blocks = [entry.astype(BF16).reshape(total, -1, entry.shape[1]) for entry in large]
    pieces = [
        jnp.moveaxis(entry.reshape(entry.shape[:-1] + (total, -1)), -2, 0).reshape(total, -1)
        for entry in small
    ]
    flat = jnp.concatenate(pieces, 1)
    room = -(-flat.shape[1] // 1024) * 1024
    packed = jnp.pad(flat, ((0, 0), (0, room - flat.shape[1]))).reshape(total, -1, 128)
    *owned, joined = scatter_blocks(blocks + [packed], sizes)
    joined = joined.reshape(-1)
    start = 0
    for entry in small:
        size = entry.size // total
        owned.append(joined[start : start + size].reshape(entry.shape[:-1] + (-1,)))
        start += size
    return tuple(owned)


def on_device(
    sizes,
    tokens,
    cotangent,
    lengths,
    qkv_weight,
    out_weight,
    up_weight,
    down_weight,
    up_bias,
    norm_gains,
    biases,
):
    is_first = lax.axis_index("section") == 0
    micro_count, own_clips, frames, width = tokens.shape
    clips = micro_count * own_clips
    own_tokens = tokens.reshape(clips * frames, width)
    own_cot = cotangent.reshape(clips * frames, width)
    visible = (jnp.arange(frames)[None, :] < lengths.reshape(clips, 1))[:, None, None, :]
    weights = gather_weights(
        (qkv_weight[0], out_weight[0], up_weight[0], down_weight[0]),
        (up_bias[0], norm_gains[0], biases[0]),
        sizes,
    )
    weights = weights[:4] + tuple(entry.astype(F32) for entry in weights[4:])

    early = layer_forward(own_tokens, visible, clips, weights)[0]
    handed = lax.ppermute(early, "section", [(0, 1)])
    source = jnp.where(is_first, own_tokens, handed)
    output, saved = layer_forward(source, visible, clips, weights)
    late = layer_backward(own_cot, saved, visible, clips, weights)[0]
    returned = lax.ppermute(late.astype(BF16), "section", [(1, 0)])
    grad_half = jnp.where(is_first, returned, own_cot)
    input_grad, grads = layer_backward(grad_half, saved, visible, clips, weights)
    owned = scatter_terms(*weight_terms(grad_half, saved, grads), sizes)
    out_shape = (1, micro_count, own_clips, frames, width)
    return (output.reshape(out_shape), input_grad.reshape(out_shape)) + tuple(
        entry[None] for entry in owned
    )


def solution(mesh):
    sizes = factor(mesh.shape["dp"])
    placed = (
        P(None, "dp", None, None),
        P(None, "dp", None, None),
        P(None, "dp"),
        P("section", "dp", None),
        P("section", "dp", None),
        P("section", "dp", None),
        P("section", "dp", None),
        P("section", "dp"),
        P("section", None, "dp"),
        P("section", None, "dp"),
    )
    return jax.shard_map(
        functools.partial(on_device, sizes),
        mesh=mesh,
        in_specs=placed,
        out_specs=(
            P("section", None, "dp", None, None),
            P("section", None, "dp", None, None),
            P("section", "dp", None),
            P("section", "dp", None),
            P("section", "dp", None),
            P("section", "dp", None),
            P("section", "dp"),
            P("section", None, "dp"),
            P("section", None, "dp"),
        ),
        check_vma=False,
    )
```

time: 1680 us -> 444 us (0.26)
  waiting for transfers between devices: 1150 us -> 1.1 us
  Pallas kernels: 0 us -> 321 us
  other arithmetic: 136 us -> 11.8 us
  blocking collectives: 123 us -> 0 us
  local copies, waits for them, and re-layouts: 121 us -> 28.6 us
  matrix products: 94.2 us -> 73.3 us
  starting transfers between devices: 22.7 us -> 2.99 us
    reduce_scatter x4 -> x0, waiting for transfers between devices: 640 us -> none  [the longest x1 177 us: on_device(): lax.psum_scatter(gradients[3][None], 'dp', scatter_dimension=1, tiled=True)]
    pallas_call x0 -> x2, Pallas kernels: none -> 321 us  [the longest x1 173 us: scatter_blocks(): pl.pallas_call(functools.partial(scatter_kernel, sizes, count), out_shape...]
    unnamed x14 -> x0, waiting for transfers between devices: 308 us -> none
    all_gather x4 -> x0, waiting for transfers between devices: 150 us -> none  [the longest x1 81.8 us: on_device(): lax.all_gather(down_weight, 'dp', axis=1, tiled=True)]
    all_gather x2 -> x0, blocking collectives: 83.6 us -> none  [the longest x1 44.9 us: on_device(): lax.all_gather(norm_gains, 'dp', axis=2, tiled=True)]
    broadcast_in_dim x5 -> x0, other arithmetic: 53.4 us -> none  [the longest x1 17.4 us: on_device(): gradients[2][None]]
    ppermute x4 -> x2, waiting for transfers between devices: 50.9 us -> 1.1 us  [the longest x1 1.04 us: on_device(): handed = lax.ppermute(early, 'section', [(0, 1)])]
    squeeze x1 -> x0, blocking collectives: 39.6 us -> none  [on_device(): weights = tuple((entry[0] for entry in gathered))]
  transfers between devices with their start and end apart: 15 -> 2, of which waited for: 10 -> 2; matrix products, arithmetic and copies ran while one was open for 14% -> 0% of each run, Pallas kernels for 0% -> 0%
where the time goes in v1:
time: 444 us; the launch traced here: 441 us
  Pallas kernels  321 us (72%)
  matrix products  73.3 us (17%)
  local copies, waits for them, and re-layouts  28.6 us (6%)
  other arithmetic  11.8 us (3%)
    pallas_call x1, Pallas kernels, scatter_blocks(): pl.pallas_call(functools.partial(scatter_kernel, sizes, count), out_shape...  173 us
    pallas_call x1, Pallas kernels, gather_blocks(): pl.pallas_call(functools.partial(gather_kernel, sizes, count), out_shape=...  148 us
    dot_general x7, matrix products, contract_cols(): lax.dot_general(left, right, (((1,), (1,)), ((), ())), preferred_element_...  28.4 us
    dot_general x4, matrix products, contract_rows(): lax.dot_general(left, right, (((0,), (0,)), ((), ())), preferred_element_...  11.1 us
    unnamed x145, local copies, waits for them, and re-layouts  10.5 us
    dot_general x2, matrix products, layer_forward(): jnp.dot(active, down_weight, preferred_element_type=F32) + biases[5]  8.93 us
  transfers between devices with their start and end apart: 2, of which 2 were waited for; matrix products, arithmetic and copies ran while one was open for 0% of the time, Pallas kernels for 0%

profile of v1, /device:TPU:0, one launch (start us, length us, event | category | flops | bytes accessed | tf_op | source)
XLA Modules:
  0.0 440.5 jit_solution(14413549216258624081)
XLA Ops:
  3.6 147.9 %gather_blocks.1 = (bf16[16,48,2304]{2,1,0:T(8,128)(2,1)}, bf16[16,48,768]{2,1,0:T(8,128)(2,1)}, bf16[16,48,3072]{2,1,0:T(8,128)(2,1)}, bf16[16,192,768]{2,1,0:T(8,128)(2,1)}, bf16[16,16,128]{2,1,0:T(8,128)(2,1)}) custom-call(bf16[48,2304]{1,0:T(8,128)(2,1)} %bitcast.253, bf16[48,768]{1,0:T(8,128)(2,1)} %bitcast.258, bf16[48,3072]{1,0:T(8,128)(2,1)} %bitcast.250, ...), custom_call_target="tpu_custom_call" | custom-call | tf_op jit(solution)/shard_map/gather_blocks/pallas_call | solution.py:148
  153.8 3.1 fusion.146
  158.1 1.9 fusion.138
  160.0 1.8 fusion.27
  163.5 6.8 %fusion.15 = bf16[256,768]{1,0:T(8,128)(2,1)S(1)} fusion(f32[256,768]{1,0:T(8,128)S(1)} %get-tuple-element.82, bf16[3072,768]{1,0:T(8,128)(2,1)} %bitcast.268, bf16[768,3072]{1,0:T(8,128)(2,1)} %bitcast.262, f32[3072]{0:T(1024)S(1)} %reshape.376, f32[768]{0:T(1024)S(1)} %add.214, f32[768]{0:T(1024)S(1)} %add.208, f32[768]{0:T(1024)S(1)} %mul.273, ...), kind=kOutput, calls=%fused_computation.49 | convolution fusion | flops 2422210560 | bytes 10640384 | tf_op jit(solution)/shard_map/dot_general | solution.py:371
  170.3 1.6 collective-permute-start
  171.9 1.0 collective-permute-done
  174.2 3.2 fusion.133
  181.6 6.1 %multiply_convert_fusion = (bf16[256,3072]{1,0:T(8,128)(2,1)}, f32[256,3072]{1,0:T(8,128)}) fusion(f32[3072]{0:T(1024)S(1)} %reshape.376, bf16[768,3072]{1,0:T(8,128)(2,1)} %bitcast.263, f32[768]{0:T(1024)S(1)} %add.208, f32[768]{0:T(1024)S(1)} %mul.273, f32[256]{0:T(256)S(1)} %add_rsqrt_fusion, f32[256,768]{1,0:T(8,128)S(1)} %get-tuple-element.86, ...), kind=kOutput, calls=%fused_computation.17 | convolution fusion | flops 1213661184 | bytes 10244096 | tf_op jit(solution)/shard_map/dot_general | solution.py:369
  187.8 8.5 %fusion.136 = (f32[256]{0:T(256)S(1)}, f32[256]{0:T(256)S(1)}, f32[256,768]{1,0:T(8,128)}) fusion(f32[256]{0:T(256)S(1)} %add_rsqrt_fusion, f32[256,768]{1,0:T(8,128)S(1)} %get-tuple-element.86, f32[256]{0:T(256)S(1)} %broadcast_multiply_fusion.8, f32[768]{0:T(1024)S(1)} %mul.273, bf16[768,3072]{1,0:T(8,128)(2,1)} %bitcast.264, ...), kind=kOutput, calls=%fused_computation.226 | convolution fusion | flops 2424962560 | bytes 14556160 | tf_op jit(solution)/shard_map/dot_general | solution.py:310
  196.3 1.6 multiply_add_fusion
  197.9 1.3 convolution_convert_fusion.9
  199.2 1.9 copy.53
  201.1 1.8 reshape.358
  202.9 1.7 multiply_reduce_fusion.1
  210.3 1.3 fusion.135
  211.9 1.4 collective-permute-start.1
  213.5 2.2 fusion.16
  216.5 11.1 %convert_reduce_fusion = (f32[3072]{0:T(1024)}, bf16[256,3072]{1,0:T(8,128)(2,1)S(1)}) fusion(f32[256,3072]{1,0:T(8,128)S(1)} %copy-done.62, bf16[256,768]{1,0:T(8,128)(2,1)S(1)} %get-tuple-element.68, bf16[3072,768]{1,0:T(8,128)(2,1)S(1)} %bitcast.273), kind=kOutput, calls=%fused_computation.16 | convolution fusion | flops 1217393664 | bytes 9842688 | tf_op jit(solution)/shard_map/dot_general | solution.py:310
  227.7 2.2 multiply_reduce_fusion.2
  231.2 1.3 convolution_convert_fusion.7
  232.4 1.9 copy.64
  234.3 1.8 reshape.362
  236.2 1.7 fusion.26
  242.3 0.9 copy-done.9
  243.3 2.8 fusion.56
  246.0 1.0 convert_reduce_fusion.1
  247.1 3.6 convolution_convert_fusion
  250.7 3.7 convolution_convert_fusion.1
  255.1 3.3 convolution_convert_fusion.2
  259.7 172.9 %scatter_blocks.1 = (f32[48,2304]{1,0:T(8,128)S(1)}, f32[48,768]{1,0:T(8,128)S(1)}, f32[48,3072]{1,0:T(8,128)S(1)}, f32[192,768]{1,0:T(8,128)S(1)}, f32[8,128]{1,0:T(8,128)S(1)}) custom-call(bf16[16,48,2304]{2,1,0:T(8,128)(2,1)} %bitcast.213, bf16[16,48,768]{2,1,0:T(8,128)(2,1)S(1)} %bitcast.202, bf16[16,48,3072]{2,1,0:T(8,128)(2,1)} %bitcast.212, ...), custom_call_target="tpu_custom_call" | custom-call | tf_op jit(solution)/shard_map/scatter_blocks/pallas_call | solution.py:282
  434.7 2.5 fusion.55
  (253 shorter events, 32.6 us)
Async XLA Ops:
  0.6 152.4 %copy-start.1 = (bf16[2,1,128,768]{3,2,1,0:T(8,128)(2,1)S(1)}, bf16[2,1,128,768]{3,2,1,0:T(8,128)(2,1)}, u32[]{:S(2)}) copy-start(bf16[2,1,128,768]{3,2,1,0:T(8,128)(2,1)} %param.10) | copy-start | bytes 1179652
  152.9 20.5 %copy-start.28 = (f32[768]{0:T(1024)}, f32[768]{0:T(1024)S(1)}, u32[]{:S(2)}) copy-start(f32[768]{0:T(1024)S(1)} %mul.266) | copy-start | bytes 9220
  153.0 20.4 %copy-start.31 = (f32[768]{0:T(1024)}, f32[768]{0:T(1024)S(1)}, u32[]{:S(2)}) copy-start(f32[768]{0:T(1024)S(1)} %add.194) | copy-start | bytes 9220
  163.3 24.4 %copy-start.33 = (f32[768]{0:T(1024)}, f32[768]{0:T(1024)S(1)}, u32[]{:S(2)}) copy-start(f32[768]{0:T(1024)S(1)} %mul.273) | copy-start | bytes 9220
  163.4 18.2 %copy-start.36 = (f32[768]{0:T(1024)}, f32[768]{0:T(1024)S(1)}, u32[]{:S(2)}) copy-start(f32[768]{0:T(1024)S(1)} %add.208) | copy-start | bytes 9220
  163.5 6.8 %copy-start.54 = (f32[768]{0:T(1024)}, f32[768]{0:T(1024)S(1)}, u32[]{:S(2)}) copy-start(f32[768]{0:T(1024)S(1)} %add.214) | copy-start | bytes 9220
  170.3 2.6 collective-permute-start
  181.3 6.4 %copy-start.41 = (f32[256]{0:T(256)}, f32[256]{0:T(256)S(1)}, u32[]{:S(2)}) copy-start(f32[256]{0:T(256)S(1)} %broadcast_multiply_fusion.8) | copy-start | bytes 3076
  181.6 6.1 %copy-start.48 = (f32[256]{0:T(256)}, f32[256]{0:T(256)S(1)}, u32[]{:S(2)}) copy-start(f32[256]{0:T(256)S(1)} %add_rsqrt_fusion) | copy-start | bytes 3076
  181.6 6.1 %copy-start.24 = (bf16[2,1,128,768]{3,2,1,0:T(8,128)(2,1)S(1)}, bf16[2,1,128,768]{3,2,1,0:T(8,128)(2,1)}, u32[]{:S(2)}) copy-start(bf16[2,1,128,768]{3,2,1,0:T(8,128)(2,1)} %param.11) | copy-start | bytes 1179652
  209.4 4.0 slice-start.2
  211.9 3.7 collective-permute-start.1
  213.4 14.2 %slice-start = ((s8[4718592]{0:T(1024)(128)(4,1)}), s8[4194304]{0:T(1024)(128)(4,1)S(1)}, s32[]{:S(2)}) async-start(s8[4718592]{0:T(1024)(128)(4,1)} %bitcast.265), calls=%async_computation | async-start | bytes 8388608
  216.4 13.4 %copy-start.6 = (bf16[256,768]{1,0:T(8,128)(2,1)}, bf16[256,768]{1,0:T(8,128)(2,1)S(1)}, u32[]{:S(2)}) copy-start(bf16[256,768]{1,0:T(8,128)(2,1)S(1)} %get-tuple-element.68) | copy-start | bytes 1179652
  216.4 11.2 %copy-start.34 = (f32[768]{0:T(1024)S(1)}, f32[768]{0:T(1024)}, u32[]{:S(2)}) copy-start(f32[768]{0:T(1024)} %copy-done.33) | copy-start | bytes 9220
  216.4 11.2 %copy-start.42 = (f32[256]{0:T(256)S(1)}, f32[256]{0:T(256)}, u32[]{:S(2)}) copy-start(f32[256]{0:T(256)} %copy-done.41) | copy-start | bytes 3076
  216.5 11.2 %copy-start.49 = (f32[256]{0:T(256)S(1)}, f32[256]{0:T(256)}, u32[]{:S(2)}) copy-start(f32[256]{0:T(256)} %copy-done.48) | copy-start | bytes 3076
  216.5 11.2 %slice-start.1 = ((s8[4718592]{0:T(1024)(128)(4,1)}), s8[524288]{0:T(1024)(128)(4,1)S(1)}, s32[]{:S(2)}) async-start(s8[4718592]{0:T(1024)(128)(4,1)} %bitcast.265), calls=%async_computation.1 | async-start | bytes 1048576
  230.8 23.6 %copy-start = (f32[256,768]{1,0:T(8,128)}, f32[256,768]{1,0:T(8,128)S(1)}, u32[]{:S(2)}) copy-start(f32[256,768]{1,0:T(8,128)S(1)} %get-tuple-element.70) | copy-start | bytes 2359300
  243.2 3.8 copy-start.7
  243.2 3.8 copy-start.17
  247.0 3.6 copy-start.27
  247.0 3.6 copy-start.35
  247.0 3.6 copy-start.37
  250.7 3.8 copy-start.23
  255.1 3.8 copy-start.44
  255.1 3.9 copy-start.52
  255.1 4.0 copy-start.56
  255.1 4.1 copy-start.51
  255.1 4.4 copy-start.53
  259.7 175.0 %copy-start.60 = (f32[256]{0:T(256)S(1)}, f32[256]{0:T(256)}, u32[]{:S(2)}) copy-start(f32[256]{0:T(256)} %get-tuple-element.50) | copy-start | bytes 3076
  259.7 175.0 %copy-start.59 = (f32[256]{0:T(256)S(1)}, f32[256]{0:T(256)}, u32[]{:S(2)}) copy-start(f32[256]{0:T(256)} %get-tuple-element.51) | copy-start | bytes 3076
  (37 other events, 64.5 us)
